TPU v7x, 256 devices: a whole 4x4x8 slice. The times are simulated.
256 devices in a mesh: band: 32 (over z, x_hi, core), kpt: 8 (over x_lo, y).
Axes of the slice: x: 4 (x_hi: 2, x_lo: 2; x = x_hi * 2 + x_lo), y: 4, z: 8, core: 2. Of those that a mesh axis runs over, the one named last changes fastest.
Arguments:
- orbitals: bfloat16 [8, 32, 2, 64000], P('kpt', 'band'), may hold values from -6 to 6
- coulomb: float32 [8, 2, 64000], P('kpt'), may hold values from 0.1 to 2
Outputs:
- exchange: float32 [8, 32, 2, 64000], P('kpt', 'band')
All inputs are finite; a program needn't handle non-finite values.
Results may differ from a plain program's by a relative error of at most 0.0085.
Values may be sent and summed in bfloat16 or wider, within the bound.
A program may use at most 64 MiB of HBM per device.

v0:
```python
import math

import jax
import jax.numpy as jnp
import ml_dtypes
import numpy as np
from jax import lax
from jax.experimental import pallas as pl
from jax.experimental.pallas import tpu as pltpu
from jax.sharding import PartitionSpec as P

NG = 40
KSTEPS = 2
BSTEPS = 2
TERMS = BSTEPS + 1
NBLOCK = 32
NK = 8
WEIGHT = -1.0 / (KSTEPS * TERMS)
BF16 = jnp.bfloat16
F32 = jnp.float32
MESH = pl.DeviceIdType.MESH
TILES = 13
ROWS = TILES * 128
CHUNKS = ((0, 7), (7, 6))


def tables():
    points = np.arange(NG)
    angle = (points[:, None] * points[None, :] % NG) * (2.0 * math.pi / NG)
    scale = 1.0 / math.sqrt(NG)
    c, s = (
        (f(angle) * scale).astype(ml_dtypes.bfloat16).astype(np.float32) for f in (np.cos, np.sin)
    )
    first = np.zeros((TERMS, 2, NG, 2, 128), np.float32)
    last = np.zeros((TERMS, 2, NG, 2, 128), np.float32)
    for t in range(TERMS):
        lanes = slice(NG * t, NG * t + NG)
        first[t, 0, :, 0, lanes] = c
        first[t, 1, :, 0, lanes] = s
        first[t, 0, :, 1, lanes] = -s
        first[t, 1, :, 1, lanes] = c
        last[t, 0, :, 0, lanes] = c
        last[t, 0, :, 1, lanes] = -s
        last[t, 1, :, 1, lanes] = c
        last[t, 1, :, 0, lanes] = s

    def rows(sign):
        table = np.zeros((2, 2, NG, 2, 2, NG), np.float32)
        for i in range(2):
            table[0, i, :, 0, i, :] = c
            table[0, i, :, 1, i, :] = sign * s
            table[1, i, :, 0, i, :] = -sign * s
            table[1, i, :, 1, i, :] = c
        return np.pad(table.reshape(160, 160), ((0, 0), (0, 96)))

    spread = np.zeros((2, 2, NG, 2, 128), np.float32)
    for s_at in range(2):
        for t in range(TERMS):
            for half in range(2):
                spread[half, s_at, points, s_at, NG * t + points] = 1
    parts = [first.reshape(240, 256), last.reshape(240, 256), rows(1.0), rows(-1.0), spread.reshape(160, 256)]
    return np.concatenate(parts, 0).astype(ml_dtypes.bfloat16)


def matrix_from_flat(flat, matrix, odd):
    for a in range(NG // 2):
        for j in range(25):
            at = 128 * (25 * a + j)
            tile = flat[:, at : at + 128].astype(F32)
            if j <= 12:
                matrix[j, pl.ds(2 * a, 2, stride=NG), :] = tile
            if j >= 12:
                odd[j - 12, pl.ds(a, 2, stride=24), :] = tile
    lane = lax.broadcasted_iota(jnp.int32, (NG // 2, 128), 1)
    for c in range(2):
        here = pltpu.roll(odd[0, 24 * c : 24 * c + 20, :], 64, 1)
        for j in range(TILES):
            after = pltpu.roll(odd[j + 1, 24 * c : 24 * c + 20, :], 64, 1) if j < 12 else here
            matrix[j, pl.ds(NG * c + 1, 20, stride=2), :] = jnp.where(lane < 64, here, after)
            here = after


def flat_from_matrix(matrix, flat, odd):
    lane = lax.broadcasted_iota(jnp.int32, (NG // 2, 128), 1)
    for c in range(2):
        before = matrix[12, pl.ds(NG * c, 20, stride=2), :]
        for j in range(TILES):
            here = pltpu.roll(matrix[j, pl.ds(NG * c + 1, 20, stride=2), :], 64, 1)
            odd[j, 24 * c : 24 * c + 20, :] = jnp.where(lane < 64, before, here)
            before = here
    for a in range(NG // 2):
        for j in range(25):
            at = 128 * (25 * a + j)
            flat[:, at : at + 128] = (
                matrix[j, pl.ds(2 * a, 2, stride=NG), :] if j < 12 else odd[j - 12, pl.ds(a, 2, stride=24), :]
            )


def dot(a, b, on):
    return lax.dot_general(a, b, ((on[:1], on[1:]), ((), ())), preferred_element_type=F32)


def spread_coulomb(matrix, spread, out):
    for j in range(TILES):
        value = matrix[j]
        high = value.astype(BF16)
        low = (value - high.astype(F32)).astype(BF16)
        both = dot(jnp.concatenate([high, low], 0), spread, (0, 0))
        out[0, 128 * j : 128 * j + 128, :] = both[:, :128]
        out[1, 128 * j : 128 * j + 128, :] = both[:, 128:]


def terms(own, visiting, coulomb, tab, total, first, fa, fb, fc, fd):
    table = lambda at, rows, cols=256: tab[at : at + rows, :cols]
    for j in range(TILES):
        a = own[j].astype(F32)
        a_re, a_im = a[:NG], a[NG:]
        parts = []
        for ref in visiting:
            b = ref[j].astype(F32)
            b_re, b_im = b[:NG], b[NG:]
            parts += [a_re * b_re + a_im * b_im, a_im * b_re - a_re * b_im]
        density = jnp.concatenate(parts, 0).astype(BF16)
        fa[128 * j : 128 * j + 128, :] = dot(density, table(0, 240), (0, 0)).astype(BF16)
    forward, inverse = table(480, 160, 160), table(640, 160, 160)
    for i in range(10):
        at = 160 * i
        a, b = fa[at : at + 80, :], fa[at + 80 : at + 160, :]
        field = jnp.concatenate(
            [jnp.concatenate([a[:, :128], b[:, :128]], 1), jnp.concatenate([a[:, 128:], b[:, 128:]], 1)], 0
        )
        r = dot(forward, field, (1, 0))
        for c in range(2):
            fb[c, at : at + 80, :] = r[80 * c : 80 * c + 80, :128]
            fb[c, at + 80 : at + 160, :] = r[80 * c : 80 * c + 80, 128:]
    for i in range(10):
        halves, scales = [], []
        for h in range(2):
            z = 4 * i + 2 * h
            halves.append(
                jnp.concatenate([fb[c, pl.ds(z + q, NG, stride=NG), :] for c in range(2) for q in range(2)], 0)
            )
            scales.append(jnp.concatenate([coulomb[pl.ds(z + q, NG, stride=NG), :] for q in range(2)] * 2, 0))
        field = jnp.concatenate(halves, 1).astype(BF16)
        r = dot(forward, field, (1, 0)).astype(BF16).astype(F32)
        scaled = (r * jnp.concatenate(scales, 1)).astype(BF16)
        r = dot(inverse, scaled, (1, 0))
        for h in range(2):
            for c in range(2):
                for q in range(2):
                    at = 80 * c + NG * q
                    fc[c, pl.ds(4 * i + 2 * h + q, NG, stride=NG), :] = r[at : at + NG, 128 * h : 128 * h + 128]
    for i in range(10):
        at = 160 * i
        field = jnp.concatenate(
            [jnp.concatenate([fc[c, at : at + 80, :], fc[c, at + 80 : at + 160, :]], 1) for c in range(2)], 0
        ).astype(BF16)
        r = dot(inverse, field, (1, 0)).astype(BF16)
        fd[at : at + 80, :] = jnp.concatenate([r[:80, :128], r[80:, :128]], 1)
        fd[at + 80 : at + 160, :] = jnp.concatenate([r[:80, 128:], r[80:, 128:]], 1)
    for j in range(TILES):
        wave = dot(table(240, 240), fd[128 * j : 128 * j + 128, :], (1, 1))
        re = im = 0.0
        for t, ref in enumerate(visiting):
            b = ref[j].astype(F32)
            b_re, b_im = b[:NG], b[NG:]
            w_re, w_im = wave[80 * t : 80 * t + NG], wave[80 * t + NG : 80 * t + 80]
            re = re + (b_re * w_re - b_im * w_im)
            im = im + (b_re * w_im + b_im * w_re)
        value = jnp.concatenate([re, im], 0)
        total[j] = value if first else (total[j] + value) * WEIGHT


def kernel(
    orbitals, coulomb, tables_ref, out,
    flat, kernel_flat, tab, matrix, kernel_matrix, odd, own, vis, total, scale, fa, fb, fc, fd, out_flat,
    local_sem, send_sem, recv_sem,
):
    n, k = lax.axis_index("band"), lax.axis_index("kpt")
    core = lax.rem(n, 2)
    sibling = n + 1 - 2 * core
    behind, ahead = lax.rem(n + NBLOCK - 2, NBLOCK), lax.rem(n + 2, NBLOCK)
    k_behind, k_ahead = lax.rem(k + NK - 1, NK), lax.rem(k + 1, NK)
    turns, turned = lax.rem(k, 4) == 3, lax.rem(k, 4) == 0

    loads = [
        pltpu.make_async_copy(orbitals.at[0, 0], flat, local_sem.at[0]),
        pltpu.make_async_copy(coulomb.at[0], kernel_flat, local_sem.at[1]),
        pltpu.make_async_copy(tables_ref, tab, local_sem.at[2]),
    ]
    for load in loads:
        load.start()
    barrier = pltpu.get_barrier_semaphore()
    for peer in ((behind, k), (n, k_behind), (sibling, k), (behind, k_behind)):
        pl.semaphore_signal(barrier, inc=1, device_id=peer, device_id_type=MESH)
    loads[0].wait()
    matrix_from_flat(flat, matrix, odd)
    own[...] = matrix[...].astype(BF16)
    pl.semaphore_wait(barrier, 4)

    used = [0]

    def copy(src, dst, peer):
        at = used[0]
        used[0] += 1
        return pltpu.make_async_remote_copy(
            src_ref=src, dst_ref=dst, send_sem=send_sem.at[at], recv_sem=recv_sem.at[at],
            device_id=peer, device_id_type=MESH,
        )

    def chunk(ref, c):
        return ref.at[pl.ds(c[0], c[1])]

    to_ahead = [copy(chunk(own, c), chunk(vis.at[0], c), (ahead, k)) for c in CHUNKS]
    to_next_k = copy(own, vis.at[2], (n, k_ahead))
    turn = copy(own, vis.at[3], (ahead, k_ahead))
    on = [copy(chunk(vis.at[0], c), chunk(vis.at[3], c), (n, k_ahead)) for c in CHUNKS]
    even_own = copy(own, vis.at[1], (sibling, k))
    even_partner = copy(vis.at[2], vis.at[4], (sibling, k))
    odd_own = [copy(chunk(vis.at[0], c), chunk(vis.at[1], c), (sibling, k)) for c in CHUNKS]
    odd_partner = [copy(chunk(vis.at[3], c), chunk(vis.at[4], c), (sibling, k)) for c in CHUNKS]

    def when(flag, *steps):
        @pl.when(flag)
        def _():
            for step in steps:
                step()

    for c in to_ahead:
        c.start()
    to_next_k.start()
    when(turns, turn.start)
    when(core == 0, even_own.start)
    loads[1].wait()
    matrix_from_flat(kernel_flat, kernel_matrix, odd)
    loads[2].wait()
    spread_coulomb(kernel_matrix, tab[800:960, :], scale)
    for i in range(2):
        to_ahead[i].wait_recv()
        when(jnp.logical_not(turns), on[i].start)
        when(core == 1, odd_own[i].start)
    to_next_k.wait_recv()
    when(core == 0, even_partner.start)
    when(core == 0, *[c.wait_recv for c in odd_own])
    when(core == 1, even_own.wait_recv)
    terms(own, [own, vis.at[1], vis.at[0]], scale.at[0], tab, total, True, fa, fb, fc, fd)
    when(turned, turn.wait_recv)
    for i in range(2):
        when(jnp.logical_not(turned), on[i].wait_recv)
        when(core == 1, odd_partner[i].start)
    when(core == 0, *[c.wait_recv for c in odd_partner])
    when(core == 1, even_partner.wait_recv)
    terms(own, [vis.at[2], vis.at[4], vis.at[3]], scale.at[1], tab, total, False, fa, fb, fc, fd)
    flat_from_matrix(total, out_flat, odd)
    store = pltpu.make_async_copy(out_flat, out.at[0, 0], local_sem.at[0])
    store.start()
    for c in to_ahead:
        c.wait_send()
    to_next_k.wait_send()
    when(turns, turn.wait_send)
    when(jnp.logical_not(turns), *[c.wait_send for c in on])
    when(core == 0, even_own.wait_send, even_partner.wait_send)
    when(core == 1, *[c.wait_send for c in odd_own + odd_partner])
    store.wait()


def shards(orbitals, coulomb):
    field = (TILES, 2 * NG, 128)
    vmem = pltpu.VMEM
    return pl.pallas_call(
        kernel,
        out_shape=jax.ShapeDtypeStruct(orbitals.shape, F32),
        in_specs=[pl.BlockSpec(memory_space=pl.ANY)] * 3,
        out_specs=pl.BlockSpec(memory_space=pl.ANY),
        scratch_shapes=[
            vmem((2, 64000), BF16), vmem((2, 64000), F32), vmem((960, 256), BF16), vmem(field, F32), vmem(field, F32),
            vmem((14, 48, 128), F32), vmem(field, BF16), vmem((5, *field), BF16), vmem(field, F32), vmem((2, ROWS, 128), F32),
            vmem((ROWS, 256), BF16), vmem((2, 1600, 128), F32), vmem((2, 1600, 128), F32), vmem((ROWS, 256), BF16),
            vmem((2, 64000), F32), pltpu.SemaphoreType.DMA((3,)), pltpu.SemaphoreType.DMA((16,)), pltpu.SemaphoreType.DMA((16,)),
        ],
        compiler_params=pltpu.CompilerParams(collective_id=0, has_side_effects=True, vmem_limit_bytes=56 << 20),
    )(orbitals, coulomb, jnp.asarray(tables()))


def solution(mesh):
    return jax.shard_map(
        shards,
        mesh=mesh,
        in_specs=(P("kpt", "band", None, None), P("kpt", None, None)),
        out_specs=P("kpt", "band", None, None),
        check_vma=False,
    )
```

profile of v0, /device:TPU:224, one launch (start us, length us, event | category | flops | bytes accessed | tf_op | source)
XLA Modules:
  0.0 31.0 jit_solution(1406403538401161120)
XLA Ops:
  0.0 29.2 %shard_map.37 = f32[1,1,2,64000]{3,2,1,0:T(2,128)} custom-call(bf16[1,1,2,64000]{3,2,1,0:T(2,128)(2,1)} %orbitals.1, f32[1,2,64000]{2,1,0:T(2,128)} %coulomb.1, bf16[960,256]{1,0:T(8,128)(2,1)} %constant.2.clone.tables_ref), custom_call_target="tpu_custom_call" | custom-call | tf_op jit(solution)/shard_map/pallas_call | solution.py:270
  29.2 1.9 %copy.5 = f32[1,1,2,64000]{3,2,1,0:T(2,128)} copy(f32[1,1,2,64000]{3,2,1,0:T(2,128)} %shard_map.37) | data formatting | bytes 1024000
where the time goes:
time: 31.2 us; the launch traced here: 31 us
  Pallas kernels  29.2 us (94%)
  local copies, waits for them, and re-layouts  1.86 us (6%)
    pallas_call x1, Pallas kernels, shards(): pl.pallas_call(kernel, out_shape=jax.ShapeDtypeStruct(orbitals.shape, F32...  29.2 us
    unnamed x1, local copies, waits for them, and re-layouts  1.86 us

commit v1 on v0

--- a/solution.py
+++ b/solution.py
@@ -173,7 +173,7 @@
 
 def kernel(
     orbitals, coulomb, tables_ref, out,
-    flat, kernel_flat, tab, matrix, kernel_matrix, odd, own, vis, total, scale, fa, fb, fc, fd, out_flat,
+    flat, kernel_flat, tab, matrix, kernel_matrix, odd, own, vis, passing, total, scale, fa, fb, fc, fd, out_flat,
     local_sem, send_sem, recv_sem,
 ):
     n, k = lax.axis_index("band"), lax.axis_index("kpt")
@@ -181,6 +181,7 @@
     sibling = n + 1 - 2 * core
     behind, ahead = lax.rem(n + NBLOCK - 2, NBLOCK), lax.rem(n + 2, NBLOCK)
     k_behind, k_ahead = lax.rem(k + NK - 1, NK), lax.rem(k + 1, NK)
+    k_beside, k_corner = lax.rem(k + 4, NK), lax.rem(k + 3, NK)
     turns, turned = lax.rem(k, 4) == 3, lax.rem(k, 4) == 0
 
     loads = [
@@ -191,20 +192,22 @@
     for load in loads:
         load.start()
     barrier = pltpu.get_barrier_semaphore()
-    for peer in ((behind, k), (n, k_behind), (sibling, k), (behind, k_behind)):
+    peers = [(behind, k), (n, k_behind), (sibling, k), (behind, k_behind), (n, k_corner), (n, k_beside), (behind, k_beside)]
+    for peer in peers:
         pl.semaphore_signal(barrier, inc=1, device_id=peer, device_id_type=MESH)
     loads[0].wait()
     matrix_from_flat(flat, matrix, odd)
     own[...] = matrix[...].astype(BF16)
-    pl.semaphore_wait(barrier, 4)
+    pl.semaphore_wait(barrier, len(peers))
 
     used = [0]
 
-    def copy(src, dst, peer):
+    def copy(src, dst, peer, arrives=None):
         at = used[0]
         used[0] += 1
+        arrives = at if arrives is None else arrives
         return pltpu.make_async_remote_copy(
-            src_ref=src, dst_ref=dst, send_sem=send_sem.at[at], recv_sem=recv_sem.at[at],
+            src_ref=src, dst_ref=dst, send_sem=send_sem.at[at], recv_sem=recv_sem.at[arrives],
             device_id=peer, device_id_type=MESH,
         )
 
@@ -212,11 +215,16 @@
         return ref.at[pl.ds(c[0], c[1])]
 
     to_ahead = [copy(chunk(own, c), chunk(vis.at[0], c), (ahead, k)) for c in CHUNKS]
-    to_next_k = copy(own, vis.at[2], (n, k_ahead))
-    turn = copy(own, vis.at[3], (ahead, k_ahead))
-    on = [copy(chunk(vis.at[0], c), chunk(vis.at[3], c), (n, k_ahead)) for c in CHUNKS]
+    to_next_k = [copy(chunk(own, c), chunk(vis.at[2], c), (n, k_ahead), 18 + i) for i, c in enumerate(CHUNKS)]
+    turn = copy(chunk(own, CHUNKS[0]), chunk(vis.at[3], CHUNKS[0]), (ahead, k_ahead), 20)
+    round_y = copy(chunk(own, CHUNKS[1]), passing, (n, lax.rem(k + 5, NK)))
+    pass_on = [
+        copy(passing, chunk(vis.at[2], CHUNKS[1]), (n, k_beside), 19),
+        copy(passing, chunk(vis.at[3], CHUNKS[1]), (ahead, k_beside), 21),
+    ]
+    on = [copy(chunk(vis.at[0], c), chunk(vis.at[3], c), (n, k_ahead), 20 + i) for i, c in enumerate(CHUNKS)]
     even_own = copy(own, vis.at[1], (sibling, k))
-    even_partner = copy(vis.at[2], vis.at[4], (sibling, k))
+    even_partner = [copy(chunk(vis.at[2], c), chunk(vis.at[4], c), (sibling, k)) for c in CHUNKS]
     odd_own = [copy(chunk(vis.at[0], c), chunk(vis.at[1], c), (sibling, k)) for c in CHUNKS]
     odd_partner = [copy(chunk(vis.at[3], c), chunk(vis.at[4], c), (sibling, k)) for c in CHUNKS]
 
@@ -226,41 +234,50 @@
             for step in steps:
                 step()
 
+    straight, both = jnp.logical_not(turns), lambda copies, name: [getattr(c, name) for c in copies]
+    when(turns, round_y.start, to_next_k[0].start, turn.start)
     for c in to_ahead:
         c.start()
-    to_next_k.start()
-    when(turns, turn.start)
+    when(straight, *both(to_next_k, "start"))
     when(core == 0, even_own.start)
     loads[1].wait()
     matrix_from_flat(kernel_flat, kernel_matrix, odd)
     loads[2].wait()
     spread_coulomb(kernel_matrix, tab[800:960, :], scale)
+    when(turned, round_y.wait_recv, *both(pass_on, "start"))
     for i in range(2):
         to_ahead[i].wait_recv()
-        when(jnp.logical_not(turns), on[i].start)
+        when(straight, on[i].start)
         when(core == 1, odd_own[i].start)
-    to_next_k.wait_recv()
-    when(core == 0, even_partner.start)
-    when(core == 0, *[c.wait_recv for c in odd_own])
+
+    def share_partner(flag):
+        @pl.when(flag)
+        def _():
+            for i in range(2):
+                to_next_k[i].wait_recv()
+                when(core == 0, even_partner[i].start)
+
+    share_partner(jnp.logical_not(turned))
+    when(core == 0, *both(odd_own, "wait_recv"))
     when(core == 1, even_own.wait_recv)
     terms(own, [own, vis.at[1], vis.at[0]], scale.at[0], tab, total, True, fa, fb, fc, fd)
-    when(turned, turn.wait_recv)
+    share_partner(turned)
     for i in range(2):
-        when(jnp.logical_not(turned), on[i].wait_recv)
+        on[i].wait_recv()
         when(core == 1, odd_partner[i].start)
-    when(core == 0, *[c.wait_recv for c in odd_partner])
-    when(core == 1, even_partner.wait_recv)
+    when(core == 0, *both(odd_partner, "wait_recv"))
+    when(core == 1, *both(even_partner, "wait_recv"))
     terms(own, [vis.at[2], vis.at[4], vis.at[3]], scale.at[1], tab, total, False, fa, fb, fc, fd)
     flat_from_matrix(total, out_flat, odd)
     store = pltpu.make_async_copy(out_flat, out.at[0, 0], local_sem.at[0])
     store.start()
     for c in to_ahead:
         c.wait_send()
-    to_next_k.wait_send()
-    when(turns, turn.wait_send)
-    when(jnp.logical_not(turns), *[c.wait_send for c in on])
-    when(core == 0, even_own.wait_send, even_partner.wait_send)
-    when(core == 1, *[c.wait_send for c in odd_own + odd_partner])
+    when(turns, round_y.wait_send, to_next_k[0].wait_send, turn.wait_send)
+    when(straight, *both(to_next_k + on, "wait_send"))
+    when(turned, *both(pass_on, "wait_send"))
+    when(core == 0, even_own.wait_send, *both(even_partner, "wait_send"))
+    when(core == 1, *both(odd_own + odd_partner, "wait_send"))
     store.wait()
 
 
@@ -274,9 +291,9 @@
         out_specs=pl.BlockSpec(memory_space=pl.ANY),
         scratch_shapes=[
             vmem((2, 64000), BF16), vmem((2, 64000), F32), vmem((960, 256), BF16), vmem(field, F32), vmem(field, F32),
-            vmem((14, 48, 128), F32), vmem(field, BF16), vmem((5, *field), BF16), vmem(field, F32), vmem((2, ROWS, 128), F32),
+            vmem((14, 48, 128), F32), vmem(field, BF16), vmem((5, *field), BF16), vmem((6, 2 * NG, 128), BF16), vmem(field, F32), vmem((2, ROWS, 128), F32),
             vmem((ROWS, 256), BF16), vmem((2, 1600, 128), F32), vmem((2, 1600, 128), F32), vmem((ROWS, 256), BF16),
-            vmem((2, 64000), F32), pltpu.SemaphoreType.DMA((3,)), pltpu.SemaphoreType.DMA((16,)), pltpu.SemaphoreType.DMA((16,)),
+            vmem((2, 64000), F32), pltpu.SemaphoreType.DMA((3,)), pltpu.SemaphoreType.DMA((18,)), pltpu.SemaphoreType.DMA((22,)),
         ],
         compiler_params=pltpu.CompilerParams(collective_id=0, has_side_effects=True, vmem_limit_bytes=56 << 20),
     )(orbitals, coulomb, jnp.asarray(tables()))

time: 31.2 us -> 30.9 us (level)
  the two profiles are of different devices: /device:TPU:224 before, /device:TPU:1 now
where the time goes in v1:
time: 30.9 us; the launch traced here: 30.7 us
  Pallas kernels  28.9 us (94%)
  local copies, waits for them, and re-layouts  1.86 us (6%)
    pallas_call x1, Pallas kernels, shards(): pl.pallas_call(kernel, out_shape=jax.ShapeDtypeStruct(orbitals.shape, F32...  28.9 us
    unnamed x1, local copies, waits for them, and re-layouts  1.86 us

profile of v1, /device:TPU:1, one launch (start us, length us, event | category | flops | bytes accessed | tf_op | source)
XLA Modules:
  0.0 30.7 jit_solution(13273212106489940516)
XLA Ops:
  0.0 28.9 %shard_map.37 = f32[1,1,2,64000]{3,2,1,0:T(2,128)} custom-call(bf16[1,1,2,64000]{3,2,1,0:T(2,128)(2,1)} %orbitals.1, f32[1,2,64000]{2,1,0:T(2,128)} %coulomb.1, bf16[960,256]{1,0:T(8,128)(2,1)} %constant.2.clone.tables_ref), custom_call_target="tpu_custom_call" | custom-call | tf_op jit(solution)/shard_map/pallas_call | solution.py:287
  28.9 1.9 %copy.5 = f32[1,1,2,64000]{3,2,1,0:T(2,128)} copy(f32[1,1,2,64000]{3,2,1,0:T(2,128)} %shard_map.37) | data formatting | bytes 1024000

commit v2 on v1

--- a/solution.py
+++ b/solution.py
@@ -13,6 +13,8 @@
 KSTEPS = 2
 BSTEPS = 2
 TERMS = BSTEPS + 1
+PAIR = 2
+STEPS_OF = ((0, 1), (0, 0), (1, 1))
 NBLOCK = 32
 NK = 8
 WEIGHT = -1.0 / (KSTEPS * TERMS)
@@ -31,9 +33,9 @@
     c, s = (
         (f(angle) * scale).astype(ml_dtypes.bfloat16).astype(np.float32) for f in (np.cos, np.sin)
     )
-    first = np.zeros((TERMS, 2, NG, 2, 128), np.float32)
-    last = np.zeros((TERMS, 2, NG, 2, 128), np.float32)
-    for t in range(TERMS):
+    first = np.zeros((PAIR, 2, NG, 2, 128), np.float32)
+    last = np.zeros((PAIR, 2, NG, 2, 128), np.float32)
+    for t in range(PAIR):
         lanes = slice(NG * t, NG * t + NG)
         first[t, 0, :, 0, lanes] = c
         first[t, 1, :, 0, lanes] = s
@@ -53,12 +55,13 @@
             table[1, i, :, 1, i, :] = c
         return np.pad(table.reshape(160, 160), ((0, 0), (0, 96)))
 
-    spread = np.zeros((2, 2, NG, 2, 128), np.float32)
-    for s_at in range(2):
-        for t in range(TERMS):
+    spread = np.zeros((2, 2, NG, 4, 128), np.float32)
+    for group, steps in enumerate(STEPS_OF):
+        for t, step in enumerate(steps):
             for half in range(2):
-                spread[half, s_at, points, s_at, NG * t + points] = 1
-    parts = [first.reshape(240, 256), last.reshape(240, 256), rows(1.0), rows(-1.0), spread.reshape(160, 256)]
+                spread[half, step, points, group, NG * t + points] = 1
+    spread = spread.reshape(160, 512)
+    parts = [first.reshape(160, 256), last.reshape(160, 256), rows(1.0), rows(-1.0), spread[:, :256], spread[:, 256:]]
     return np.concatenate(parts, 0).astype(ml_dtypes.bfloat16)
 
 
@@ -100,20 +103,22 @@
     return lax.dot_general(a, b, ((on[:1], on[1:]), ((), ())), preferred_element_type=F32)
 
 
-def spread_coulomb(matrix, spread, out):
+def spread_coulomb(matrix, tab, out):
     for j in range(TILES):
         value = matrix[j]
         high = value.astype(BF16)
         low = (value - high.astype(F32)).astype(BF16)
-        both = dot(jnp.concatenate([high, low], 0), spread, (0, 0))
+        value = jnp.concatenate([high, low], 0)
+        both = dot(value, tab[640:800, :], (0, 0))
         out[0, 128 * j : 128 * j + 128, :] = both[:, :128]
         out[1, 128 * j : 128 * j + 128, :] = both[:, 128:]
-
-
-def terms(own, visiting, coulomb, tab, total, first, fa, fb, fc, fd):
+        out[2, 128 * j : 128 * j + 128, :] = dot(value, tab[800:960, :128], (0, 0))
+
+
+def terms(block, visiting, coulomb, tab, total, last, fa, fb, fc, fd):
     table = lambda at, rows, cols=256: tab[at : at + rows, :cols]
     for j in range(TILES):
-        a = own[j].astype(F32)
+        a = block[j].astype(F32)
         a_re, a_im = a[:NG], a[NG:]
         parts = []
         for ref in visiting:
@@ -121,8 +126,8 @@
             b_re, b_im = b[:NG], b[NG:]
             parts += [a_re * b_re + a_im * b_im, a_im * b_re - a_re * b_im]
         density = jnp.concatenate(parts, 0).astype(BF16)
-        fa[128 * j : 128 * j + 128, :] = dot(density, table(0, 240), (0, 0)).astype(BF16)
-    forward, inverse = table(480, 160, 160), table(640, 160, 160)
+        fa[128 * j : 128 * j + 128, :] = dot(density, table(0, 160), (0, 0)).astype(BF16)
+    forward, inverse = table(320, 160, 160), table(480, 160, 160)
     for i in range(10):
         at = 160 * i
         a, b = fa[at : at + 80, :], fa[at + 80 : at + 160, :]
@@ -159,7 +164,7 @@
         fd[at : at + 80, :] = jnp.concatenate([r[:80, :128], r[80:, :128]], 1)
         fd[at + 80 : at + 160, :] = jnp.concatenate([r[:80, 128:], r[80:, 128:]], 1)
     for j in range(TILES):
-        wave = dot(table(240, 240), fd[128 * j : 128 * j + 128, :], (1, 1))
+        wave = dot(table(160, 160), fd[128 * j : 128 * j + 128, :], (1, 1))
         re = im = 0.0
         for t, ref in enumerate(visiting):
             b = ref[j].astype(F32)
@@ -168,12 +173,12 @@
             re = re + (b_re * w_re - b_im * w_im)
             im = im + (b_re * w_im + b_im * w_re)
         value = jnp.concatenate([re, im], 0)
-        total[j] = value if first else (total[j] + value) * WEIGHT
+        total[j] = (total[j] + value) * WEIGHT if last else total[j] + value
 
 
 def kernel(
     orbitals, coulomb, tables_ref, out,
-    flat, kernel_flat, tab, matrix, kernel_matrix, odd, own, vis, passing, total, scale, fa, fb, fc, fd, out_flat,
+    flat, kernel_flat, tab, matrix, kernel_matrix, odd, vis, passing, total, scale, fa, fb, fc, fd, out_flat,
     local_sem, send_sem, recv_sem,
 ):
     n, k = lax.axis_index("band"), lax.axis_index("kpt")
@@ -182,6 +187,7 @@
     behind, ahead = lax.rem(n + NBLOCK - 2, NBLOCK), lax.rem(n + 2, NBLOCK)
     k_behind, k_ahead = lax.rem(k + NK - 1, NK), lax.rem(k + 1, NK)
     k_beside, k_corner = lax.rem(k + 4, NK), lax.rem(k + 3, NK)
+    late, on_time, to_late = n < 2, n >= 2, n >= NBLOCK - 2
     turns, turned = lax.rem(k, 4) == 3, lax.rem(k, 4) == 0
 
     loads = [
@@ -192,12 +198,12 @@
     for load in loads:
         load.start()
     barrier = pltpu.get_barrier_semaphore()
-    peers = [(behind, k), (n, k_behind), (sibling, k), (behind, k_behind), (n, k_corner), (n, k_beside), (behind, k_beside)]
+    peers = [(behind, k), (n, k_behind), (sibling, k), (n, k_corner), (n, k_beside), (behind, k_beside)]
     for peer in peers:
         pl.semaphore_signal(barrier, inc=1, device_id=peer, device_id_type=MESH)
     loads[0].wait()
     matrix_from_flat(flat, matrix, odd)
-    own[...] = matrix[...].astype(BF16)
+    vis[0] = matrix[...].astype(BF16)
     pl.semaphore_wait(barrier, len(peers))
 
     used = [0]
@@ -214,19 +220,22 @@
     def chunk(ref, c):
         return ref.at[pl.ds(c[0], c[1])]
 
-    to_ahead = [copy(chunk(own, c), chunk(vis.at[0], c), (ahead, k)) for c in CHUNKS]
-    to_next_k = [copy(chunk(own, c), chunk(vis.at[2], c), (n, k_ahead), 18 + i) for i, c in enumerate(CHUNKS)]
-    turn = copy(chunk(own, CHUNKS[0]), chunk(vis.at[3], CHUNKS[0]), (ahead, k_ahead), 20)
-    round_y = copy(chunk(own, CHUNKS[1]), passing, (n, lax.rem(k + 5, NK)))
+    def copies(src, dst, peer, arrives=None):
+        arrives = (None, None) if arrives is None else (arrives, arrives + 1)
+        return [copy(chunk(vis.at[src], c), chunk(vis.at[dst], c), peer, at) for c, at in zip(CHUNKS, arrives)]
+
+    to_ahead = copies(0, 3, (ahead, k))
+    to_next_k = copies(0, 1, (n, k_ahead), 24)
+    on_x = copies(1, 5, (ahead, k), 26)
+    on_y = copy(chunk(vis.at[3], CHUNKS[0]), chunk(vis.at[5], CHUNKS[0]), (n, k_ahead), 26)
+    round_y = [copy(chunk(vis.at[0], c), chunk(passing, c), (n, lax.rem(k + 5, NK))) for c in CHUNKS]
     pass_on = [
-        copy(passing, chunk(vis.at[2], CHUNKS[1]), (n, k_beside), 19),
-        copy(passing, chunk(vis.at[3], CHUNKS[1]), (ahead, k_beside), 21),
+        copy(chunk(passing, c), chunk(vis.at[dst], c), peer, at + i)
+        for i, c in enumerate(CHUNKS)
+        for dst, peer, at in ((1, (n, k_beside), 24), (5, (ahead, k_beside), 26))
     ]
-    on = [copy(chunk(vis.at[0], c), chunk(vis.at[3], c), (n, k_ahead), 20 + i) for i, c in enumerate(CHUNKS)]
-    even_own = copy(own, vis.at[1], (sibling, k))
-    even_partner = [copy(chunk(vis.at[2], c), chunk(vis.at[4], c), (sibling, k)) for c in CHUNKS]
-    odd_own = [copy(chunk(vis.at[0], c), chunk(vis.at[1], c), (sibling, k)) for c in CHUNKS]
-    odd_partner = [copy(chunk(vis.at[3], c), chunk(vis.at[4], c), (sibling, k)) for c in CHUNKS]
+    even_own, even_partner = copies(0, 2, (sibling, k)), copies(1, 4, (sibling, k))
+    odd_own, odd_partner = copies(3, 2, (sibling, k)), copies(5, 4, (sibling, k))
 
     def when(flag, *steps):
         @pl.when(flag)
@@ -234,49 +243,77 @@
             for step in steps:
                 step()
 
-    straight, both = jnp.logical_not(turns), lambda copies, name: [getattr(c, name) for c in copies]
-    when(turns, round_y.start, to_next_k[0].start, turn.start)
+    def both(copies, name):
+        return [getattr(c, name) for c in copies]
+
+    straight, inner = jnp.logical_not(turns), jnp.logical_not(turned)
+    when(turns, round_y[0].start)
     for c in to_ahead:
         c.start()
     when(straight, *both(to_next_k, "start"))
-    when(core == 0, even_own.start)
+    when(core == 0, *both(even_own, "start"))
+    total[...] = jnp.zeros_like(total)
     loads[1].wait()
     matrix_from_flat(kernel_flat, kernel_matrix, odd)
     loads[2].wait()
-    spread_coulomb(kernel_matrix, tab[800:960, :], scale)
-    when(turned, round_y.wait_recv, *both(pass_on, "start"))
+    spread_coulomb(kernel_matrix, tab, scale)
+    when(turns, round_y[0].wait_send, round_y[1].start)
     for i in range(2):
-        to_ahead[i].wait_recv()
-        when(straight, on[i].start)
-        when(core == 1, odd_own[i].start)
-
-    def share_partner(flag):
+        when(turned, round_y[i].wait_recv, *both(pass_on[2 * i : 2 * i + 2], "start"))
+
+    def partner(flag):
         @pl.when(flag)
         def _():
             for i in range(2):
                 to_next_k[i].wait_recv()
+                when(inner if i == 1 else inner & to_late, on_x[i].start)
                 when(core == 0, even_partner[i].start)
 
-    share_partner(jnp.logical_not(turned))
-    when(core == 0, *both(odd_own, "wait_recv"))
-    when(core == 1, even_own.wait_recv)
-    terms(own, [own, vis.at[1], vis.at[0]], scale.at[0], tab, total, True, fa, fb, fc, fd)
-    share_partner(turned)
+    def block_behind(flag):
+        @pl.when(flag)
+        def _():
+            for i in range(2):
+                to_ahead[i].wait_recv()
+                if i == 0:
+                    when(straight & on_time, on_y.start)
+                when(core == 1, odd_own[i].start)
+
+    def from_sibling(flag):
+        when(flag & (core == 0), *both(odd_own, "wait_recv"))
+        when(flag & (core == 1), *both(even_own, "wait_recv"))
+
+    def add(group, last=False):
+        pair = [vis.at[2 * group], vis.at[2 * group + 1]]
+        terms(vis.at[0], pair, scale.at[group], tab, total, last, fa, fb, fc, fd)
+
+    swap, keep = turned & on_time, jnp.logical_not(turned & on_time)
+    partner(inner)
+    block_behind(on_time)
+    partner(turned & late)
+    from_sibling(swap)
+    add(lax.select(swap, 1, 0))
+    partner(swap)
+    block_behind(late)
+    from_sibling(keep)
+    add(lax.select(swap, 0, 1))
     for i in range(2):
-        on[i].wait_recv()
+        on_x[i].wait_recv()
         when(core == 1, odd_partner[i].start)
     when(core == 0, *both(odd_partner, "wait_recv"))
     when(core == 1, *both(even_partner, "wait_recv"))
-    terms(own, [vis.at[2], vis.at[4], vis.at[3]], scale.at[1], tab, total, False, fa, fb, fc, fd)
+    add(2, True)
     flat_from_matrix(total, out_flat, odd)
     store = pltpu.make_async_copy(out_flat, out.at[0, 0], local_sem.at[0])
     store.start()
     for c in to_ahead:
         c.wait_send()
-    when(turns, round_y.wait_send, to_next_k[0].wait_send, turn.wait_send)
-    when(straight, *both(to_next_k + on, "wait_send"))
+    when(turns, round_y[1].wait_send)
+    when(straight, *both(to_next_k, "wait_send"))
+    when(inner, on_x[1].wait_send)
+    when(inner & to_late, on_x[0].wait_send)
+    when(straight & on_time, on_y.wait_send)
     when(turned, *both(pass_on, "wait_send"))
-    when(core == 0, even_own.wait_send, *both(even_partner, "wait_send"))
+    when(core == 0, *both(even_own + even_partner, "wait_send"))
     when(core == 1, *both(odd_own + odd_partner, "wait_send"))
     store.wait()
 
@@ -291,9 +328,9 @@
         out_specs=pl.BlockSpec(memory_space=pl.ANY),
         scratch_shapes=[
             vmem((2, 64000), BF16), vmem((2, 64000), F32), vmem((960, 256), BF16), vmem(field, F32), vmem(field, F32),
-            vmem((14, 48, 128), F32), vmem(field, BF16), vmem((5, *field), BF16), vmem((6, 2 * NG, 128), BF16), vmem(field, F32), vmem((2, ROWS, 128), F32),
+            vmem((14, 48, 128), F32), vmem((6, *field), BF16), vmem(field, BF16), vmem(field, F32), vmem((3, ROWS, 128), F32),
             vmem((ROWS, 256), BF16), vmem((2, 1600, 128), F32), vmem((2, 1600, 128), F32), vmem((ROWS, 256), BF16),
-            vmem((2, 64000), F32), pltpu.SemaphoreType.DMA((3,)), pltpu.SemaphoreType.DMA((18,)), pltpu.SemaphoreType.DMA((22,)),
+            vmem((2, 64000), F32), pltpu.SemaphoreType.DMA((3,)), pltpu.SemaphoreType.DMA((24,)), pltpu.SemaphoreType.DMA((28,)),
         ],
         compiler_params=pltpu.CompilerParams(collective_id=0, has_side_effects=True, vmem_limit_bytes=56 << 20),
     )(orbitals, coulomb, jnp.asarray(tables()))

time: 30.9 us -> 28.9 us (0.935)
  the two profiles are of different devices: /device:TPU:1 before, /device:TPU:6 now
where the time goes in v2:
time: 28.9 us; the launch traced here: 28.8 us
  Pallas kernels  26.9 us (93%)
  local copies, waits for them, and re-layouts  1.86 us (6%)
    pallas_call x1, Pallas kernels, shards(): pl.pallas_call(kernel, out_shape=jax.ShapeDtypeStruct(orbitals.shape, F32...  26.9 us
    unnamed x1, local copies, waits for them, and re-layouts  1.86 us

profile of v2, /device:TPU:6, one launch (start us, length us, event | category | flops | bytes accessed | tf_op | source)
XLA Modules:
  0.0 28.8 jit_solution(6790759385794822449)
XLA Ops:
  0.0 26.9 %shard_map.37 = f32[1,1,2,64000]{3,2,1,0:T(2,128)} custom-call(bf16[1,1,2,64000]{3,2,1,0:T(2,128)(2,1)} %orbitals.1, f32[1,2,64000]{2,1,0:T(2,128)} %coulomb.1, bf16[960,256]{1,0:T(8,128)(2,1)} %constant.2.clone.tables_ref), custom_call_target="tpu_custom_call" | custom-call | tf_op jit(solution)/shard_map/pallas_call | solution.py:324
  26.9 1.9 %copy.5 = f32[1,1,2,64000]{3,2,1,0:T(2,128)} copy(f32[1,1,2,64000]{3,2,1,0:T(2,128)} %shard_map.37) | data formatting | bytes 1024000

commit v3 on v2

--- a/solution.py
+++ b/solution.py
@@ -83,7 +83,7 @@
             here = after
 
 
-def flat_from_matrix(matrix, flat, odd):
+def flat_from_matrix(matrix, flat, odd, done):
     lane = lax.broadcasted_iota(jnp.int32, (NG // 2, 128), 1)
     for c in range(2):
         before = matrix[12, pl.ds(NG * c, 20, stride=2), :]
@@ -97,6 +97,7 @@
             flat[:, at : at + 128] = (
                 matrix[j, pl.ds(2 * a, 2, stride=NG), :] if j < 12 else odd[j - 12, pl.ds(a, 2, stride=24), :]
             )
+        done(a)
 
 
 def dot(a, b, on):
@@ -177,8 +178,8 @@
 
 
 def kernel(
-    orbitals, coulomb, tables_ref, out,
-    flat, kernel_flat, tab, matrix, kernel_matrix, odd, vis, passing, total, scale, fa, fb, fc, fd, out_flat,
+    orbitals, coulomb, tables_ref, total,
+    flat, kernel_flat, tab, matrix, kernel_matrix, odd, vis, passing, scale, fa, fb, fc, fd,
     local_sem, send_sem, recv_sem,
 ):
     n, k = lax.axis_index("band"), lax.axis_index("kpt")
@@ -187,7 +188,7 @@
     behind, ahead = lax.rem(n + NBLOCK - 2, NBLOCK), lax.rem(n + 2, NBLOCK)
     k_behind, k_ahead = lax.rem(k + NK - 1, NK), lax.rem(k + 1, NK)
     k_beside, k_corner = lax.rem(k + 4, NK), lax.rem(k + 3, NK)
-    late, on_time, to_late = n < 2, n >= 2, n >= NBLOCK - 2
+    late, on_time = n < 2, n >= 2
     turns, turned = lax.rem(k, 4) == 3, lax.rem(k, 4) == 0
 
     loads = [
@@ -226,7 +227,7 @@
 
     to_ahead = copies(0, 3, (ahead, k))
     to_next_k = copies(0, 1, (n, k_ahead), 24)
-    on_x = copies(1, 5, (ahead, k), 26)
+    on_x = copy(chunk(vis.at[1], CHUNKS[1]), chunk(vis.at[5], CHUNKS[1]), (ahead, k), 27)
     on_y = copy(chunk(vis.at[3], CHUNKS[0]), chunk(vis.at[5], CHUNKS[0]), (n, k_ahead), 26)
     round_y = [copy(chunk(vis.at[0], c), chunk(passing, c), (n, lax.rem(k + 5, NK))) for c in CHUNKS]
     pass_on = [
@@ -248,9 +249,8 @@
 
     straight, inner = jnp.logical_not(turns), jnp.logical_not(turned)
     when(turns, round_y[0].start)
-    for c in to_ahead:
-        c.start()
-    when(straight, *both(to_next_k, "start"))
+    to_ahead[0].start()
+    when(straight, to_next_k[1].start)
     when(core == 0, *both(even_own, "start"))
     total[...] = jnp.zeros_like(total)
     loads[1].wait()
@@ -258,25 +258,27 @@
     loads[2].wait()
     spread_coulomb(kernel_matrix, tab, scale)
     when(turns, round_y[0].wait_send, round_y[1].start)
+    when(straight, to_next_k[1].wait_send, to_next_k[0].start)
+    to_ahead[0].wait_send()
+    to_ahead[1].start()
     for i in range(2):
         when(turned, round_y[i].wait_recv, *both(pass_on[2 * i : 2 * i + 2], "start"))
 
-    def partner(flag):
+    def partner(i, flag):
         @pl.when(flag)
         def _():
-            for i in range(2):
-                to_next_k[i].wait_recv()
-                when(inner if i == 1 else inner & to_late, on_x[i].start)
-                when(core == 0, even_partner[i].start)
-
-    def block_behind(flag):
+            to_next_k[i].wait_recv()
+            if i == 1:
+                when(inner, on_x.start)
+            when(core == 0, even_partner[i].start)
+
+    def block_behind(i, flag):
         @pl.when(flag)
         def _():
-            for i in range(2):
-                to_ahead[i].wait_recv()
-                if i == 0:
-                    when(straight & on_time, on_y.start)
-                when(core == 1, odd_own[i].start)
+            to_ahead[i].wait_recv()
+            if i == 0:
+                when(straight, on_y.start)
+            when(core == 1, odd_own[i].start)
 
     def from_sibling(flag):
         when(flag & (core == 0), *both(odd_own, "wait_recv"))
@@ -287,53 +289,74 @@
         terms(vis.at[0], pair, scale.at[group], tab, total, last, fa, fb, fc, fd)
 
     swap, keep = turned & on_time, jnp.logical_not(turned & on_time)
-    partner(inner)
-    block_behind(on_time)
-    partner(turned & late)
+    partner(1, inner)
+    block_behind(0, on_time)
+    partner(0, inner)
+    block_behind(1, on_time)
+    partner(0, turned & late)
+    partner(1, turned & late)
     from_sibling(swap)
     add(lax.select(swap, 1, 0))
-    partner(swap)
-    block_behind(late)
+    partner(0, swap)
+    partner(1, swap)
+    block_behind(0, late)
+    block_behind(1, late)
     from_sibling(keep)
     add(lax.select(swap, 0, 1))
-    for i in range(2):
-        on_x[i].wait_recv()
+    for i, arrived in enumerate((on_y, on_x)):
+        arrived.wait_recv()
         when(core == 1, odd_partner[i].start)
     when(core == 0, *both(odd_partner, "wait_recv"))
     when(core == 1, *both(even_partner, "wait_recv"))
     add(2, True)
-    flat_from_matrix(total, out_flat, odd)
-    store = pltpu.make_async_copy(out_flat, out.at[0, 0], local_sem.at[0])
-    store.start()
-    for c in to_ahead:
-        c.wait_send()
+    to_ahead[1].wait_send()
     when(turns, round_y[1].wait_send)
-    when(straight, *both(to_next_k, "wait_send"))
-    when(inner, on_x[1].wait_send)
-    when(inner & to_late, on_x[0].wait_send)
-    when(straight & on_time, on_y.wait_send)
+    when(straight, to_next_k[0].wait_send, on_y.wait_send)
+    when(inner, on_x.wait_send)
     when(turned, *both(pass_on, "wait_send"))
     when(core == 0, *both(even_own + even_partner, "wait_send"))
     when(core == 1, *both(odd_own + odd_partner, "wait_send"))
-    store.wait()
+
+
+def write(total, out, odd, flat, sem):
+    stores = [
+        pltpu.make_async_copy(flat.at[:, pl.ds(at, 16000)], out.at[0, 0, :, pl.ds(at, 16000)], sem.at[i])
+        for i, at in enumerate(range(0, 64000, 16000))
+    ]
+
+    def done(a):
+        if a % 5 == 4:
+            stores[a // 5].start()
+
+    flat_from_matrix(total, flat, odd, done)
+    for store in stores:
+        store.wait()
 
 
 def shards(orbitals, coulomb):
     field = (TILES, 2 * NG, 128)
     vmem = pltpu.VMEM
-    return pl.pallas_call(
+    total = pl.pallas_call(
         kernel,
-        out_shape=jax.ShapeDtypeStruct(orbitals.shape, F32),
+        out_shape=pltpu.VMEM(field, F32),
         in_specs=[pl.BlockSpec(memory_space=pl.ANY)] * 3,
-        out_specs=pl.BlockSpec(memory_space=pl.ANY),
+        out_specs=pl.BlockSpec(memory_space=pltpu.VMEM),
         scratch_shapes=[
             vmem((2, 64000), BF16), vmem((2, 64000), F32), vmem((960, 256), BF16), vmem(field, F32), vmem(field, F32),
-            vmem((14, 48, 128), F32), vmem((6, *field), BF16), vmem(field, BF16), vmem(field, F32), vmem((3, ROWS, 128), F32),
+            vmem((14, 48, 128), F32), vmem((6, *field), BF16), vmem(field, BF16), vmem((3, ROWS, 128), F32),
             vmem((ROWS, 256), BF16), vmem((2, 1600, 128), F32), vmem((2, 1600, 128), F32), vmem((ROWS, 256), BF16),
-            vmem((2, 64000), F32), pltpu.SemaphoreType.DMA((3,)), pltpu.SemaphoreType.DMA((24,)), pltpu.SemaphoreType.DMA((28,)),
+            pltpu.SemaphoreType.DMA((3,)), pltpu.SemaphoreType.DMA((24,)), pltpu.SemaphoreType.DMA((28,)),
         ],
         compiler_params=pltpu.CompilerParams(collective_id=0, has_side_effects=True, vmem_limit_bytes=56 << 20),
     )(orbitals, coulomb, jnp.asarray(tables()))
+    return pl.pallas_call(
+        write,
+        out_shape=jax.ShapeDtypeStruct(orbitals.shape, F32),
+        in_specs=[pl.BlockSpec(memory_space=pltpu.VMEM)],
+        out_specs=pl.BlockSpec(memory_space=pl.ANY),
+        scratch_shapes=[vmem((14, 48, 128), F32), vmem((2, 64000), F32), pltpu.SemaphoreType.DMA((4,))],
+        compiler_params=pltpu.CompilerParams(vmem_limit_bytes=16 << 20),
+    )(total)
 
 
 def solution(mesh):

time: 28.9 us -> 27 us (0.934)
  the two profiles are of different devices: /device:TPU:6 before, /device:TPU:4 now
where the time goes in v3:
time: 27 us; the launch traced here: 26.9 us
  Pallas kernels  26.9 us (100%)
    pallas_call x1, Pallas kernels, shards(): pl.pallas_call(kernel, out_shape=pltpu.VMEM(field, F32), in_specs=[pl.Blo...  25.9 us
    pallas_call x1, Pallas kernels, shards(): pl.pallas_call(write, out_shape=jax.ShapeDtypeStruct(orbitals.shape, F32)...  1.04 us

profile of v3, /device:TPU:4, one launch (start us, length us, event | category | flops | bytes accessed | tf_op | source)
XLA Modules:
  0.0 26.9 jit_solution(5353276847268536111)
XLA Ops:
  0.0 25.9 %shard_map.37.total = f32[13,80,128]{2,1,0:T(8,128)S(1)} custom-call(bf16[1,1,2,64000]{3,2,1,0:T(2,128)(2,1)} %orbitals.1, f32[1,2,64000]{2,1,0:T(2,128)} %coulomb.1, bf16[960,256]{1,0:T(8,128)(2,1)} %constant.2.clone.tables_ref), custom_call_target="tpu_custom_call" | custom-call | tf_op jit(solution)/shard_map/pallas_call | solution.py:339
  25.9 1.0 %shard_map.38 = f32[1,1,2,64000]{3,2,1,0:T(2,128)} custom-call(f32[13,80,128]{2,1,0:T(8,128)S(1)} %shard_map.37.total), custom_call_target="tpu_custom_call" | custom-call | tf_op jit(solution)/shard_map/pallas_call | solution.py:352

commit v4 on v3

--- a/solution.py
+++ b/solution.py
@@ -13,8 +13,7 @@
 KSTEPS = 2
 BSTEPS = 2
 TERMS = BSTEPS + 1
-PAIR = 2
-STEPS_OF = ((0, 1), (0, 0), (1, 1))
+STEPS_OF = ((0, 0, 0), (1, 1, 1), (0, 1, 1))
 NBLOCK = 32
 NK = 8
 WEIGHT = -1.0 / (KSTEPS * TERMS)
@@ -33,9 +32,9 @@
     c, s = (
         (f(angle) * scale).astype(ml_dtypes.bfloat16).astype(np.float32) for f in (np.cos, np.sin)
     )
-    first = np.zeros((PAIR, 2, NG, 2, 128), np.float32)
-    last = np.zeros((PAIR, 2, NG, 2, 128), np.float32)
-    for t in range(PAIR):
+    first = np.zeros((TERMS, 2, NG, 2, 128), np.float32)
+    last = np.zeros((TERMS, 2, NG, 2, 128), np.float32)
+    for t in range(TERMS):
         lanes = slice(NG * t, NG * t + NG)
         first[t, 0, :, 0, lanes] = c
         first[t, 1, :, 0, lanes] = s
@@ -61,7 +60,7 @@
             for half in range(2):
                 spread[half, step, points, group, NG * t + points] = 1
     spread = spread.reshape(160, 512)
-    parts = [first.reshape(160, 256), last.reshape(160, 256), rows(1.0), rows(-1.0), spread[:, :256], spread[:, 256:]]
+    parts = [first.reshape(240, 256), last.reshape(240, 256), rows(1.0), rows(-1.0), spread[:, :256], spread[:, 256:]]
     return np.concatenate(parts, 0).astype(ml_dtypes.bfloat16)
 
 
@@ -110,14 +109,15 @@
         high = value.astype(BF16)
         low = (value - high.astype(F32)).astype(BF16)
         value = jnp.concatenate([high, low], 0)
-        both = dot(value, tab[640:800, :], (0, 0))
+        both = dot(value, tab[800:960, :], (0, 0))
         out[0, 128 * j : 128 * j + 128, :] = both[:, :128]
         out[1, 128 * j : 128 * j + 128, :] = both[:, 128:]
-        out[2, 128 * j : 128 * j + 128, :] = dot(value, tab[800:960, :128], (0, 0))
+        out[2, 128 * j : 128 * j + 128, :] = dot(value, tab[960:1120, :128], (0, 0))
 
 
 def terms(block, visiting, coulomb, tab, total, last, fa, fb, fc, fd):
     table = lambda at, rows, cols=256: tab[at : at + rows, :cols]
+    rows = 2 * NG * len(visiting)
     for j in range(TILES):
         a = block[j].astype(F32)
         a_re, a_im = a[:NG], a[NG:]
@@ -127,8 +127,8 @@
             b_re, b_im = b[:NG], b[NG:]
             parts += [a_re * b_re + a_im * b_im, a_im * b_re - a_re * b_im]
         density = jnp.concatenate(parts, 0).astype(BF16)
-        fa[128 * j : 128 * j + 128, :] = dot(density, table(0, 160), (0, 0)).astype(BF16)
-    forward, inverse = table(320, 160, 160), table(480, 160, 160)
+        fa[128 * j : 128 * j + 128, :] = dot(density, table(0, rows), (0, 0)).astype(BF16)
+    forward, inverse = table(480, 160, 160), table(640, 160, 160)
     for i in range(10):
         at = 160 * i
         a, b = fa[at : at + 80, :], fa[at + 80 : at + 160, :]
@@ -165,7 +165,7 @@
         fd[at : at + 80, :] = jnp.concatenate([r[:80, :128], r[80:, :128]], 1)
         fd[at + 80 : at + 160, :] = jnp.concatenate([r[:80, 128:], r[80:, 128:]], 1)
     for j in range(TILES):
-        wave = dot(table(160, 160), fd[128 * j : 128 * j + 128, :], (1, 1))
+        wave = dot(table(240, rows), fd[128 * j : 128 * j + 128, :], (1, 1))
         re = im = 0.0
         for t, ref in enumerate(visiting):
             b = ref[j].astype(F32)
@@ -191,6 +191,15 @@
     late, on_time = n < 2, n >= 2
     turns, turned = lax.rem(k, 4) == 3, lax.rem(k, 4) == 0
 
+    barrier = pltpu.get_barrier_semaphore()
+
+    def ready(*peers):
+        for peer in peers:
+            pl.semaphore_signal(barrier, inc=1, device_id=peer, device_id_type=MESH)
+
+    ready((behind, k), (sibling, k))
+    pl.when(jnp.logical_not(turned))(lambda: ready((n, k_behind)))
+    pl.when(turned)(lambda: ready((n, k_corner), (n, k_beside), (behind, k_beside)))
     loads = [
         pltpu.make_async_copy(orbitals.at[0, 0], flat, local_sem.at[0]),
         pltpu.make_async_copy(coulomb.at[0], kernel_flat, local_sem.at[1]),
@@ -198,14 +207,10 @@
     ]
     for load in loads:
         load.start()
-    barrier = pltpu.get_barrier_semaphore()
-    peers = [(behind, k), (n, k_behind), (sibling, k), (n, k_corner), (n, k_beside), (behind, k_beside)]
-    for peer in peers:
-        pl.semaphore_signal(barrier, inc=1, device_id=peer, device_id_type=MESH)
     loads[0].wait()
     matrix_from_flat(flat, matrix, odd)
-    vis[0] = matrix[...].astype(BF16)
-    pl.semaphore_wait(barrier, len(peers))
+    vis[0] = matrix[:TILES].astype(BF16)
+    pl.semaphore_wait(barrier, 3 + 2 * turned.astype(jnp.int32))
 
     used = [0]
 
@@ -250,19 +255,24 @@
     straight, inner = jnp.logical_not(turns), jnp.logical_not(turned)
     when(turns, round_y[0].start)
     to_ahead[0].start()
+    at_once = n >= NBLOCK - 2
+    when(at_once, to_ahead[1].start)
     when(straight, to_next_k[1].start)
     when(core == 0, *both(even_own, "start"))
-    total[...] = jnp.zeros_like(total)
+    total[:TILES] = jnp.zeros((TILES, 2 * NG, 128), F32)
     loads[1].wait()
     matrix_from_flat(kernel_flat, kernel_matrix, odd)
     loads[2].wait()
     spread_coulomb(kernel_matrix, tab, scale)
     when(turns, round_y[0].wait_send, round_y[1].start)
     when(straight, to_next_k[1].wait_send, to_next_k[0].start)
-    to_ahead[0].wait_send()
-    to_ahead[1].start()
+    when(jnp.logical_not(at_once), to_ahead[0].wait_send, to_ahead[1].start)
+    @pl.when(turned)
+    def _():
+        terms(vis.at[0], [vis.at[0]], scale.at[0], tab, total, False, fa, fb, fc, fd)
+
     for i in range(2):
-        when(turned, round_y[i].wait_recv, *both(pass_on[2 * i : 2 * i + 2], "start"))
+        when(turned, round_y[i].wait_recv, pass_on[2 * i + 1].start, pass_on[2 * i].start)
 
     def partner(i, flag):
         @pl.when(flag)
@@ -280,35 +290,34 @@
                 when(straight, on_y.start)
             when(core == 1, odd_own[i].start)
 
-    def from_sibling(flag):
-        when(flag & (core == 0), *both(odd_own, "wait_recv"))
-        when(flag & (core == 1), *both(even_own, "wait_recv"))
-
-    def add(group, last=False):
-        pair = [vis.at[2 * group], vis.at[2 * group + 1]]
-        terms(vis.at[0], pair, scale.at[group], tab, total, last, fa, fb, fc, fd)
-
-    swap, keep = turned & on_time, jnp.logical_not(turned & on_time)
+    early = turned | on_time
+
+    def add(slots, steps, flag=None, last=False):
+        def work():
+            terms(vis.at[0], [vis.at[i] for i in slots], scale.at[steps], tab, total, last, fa, fb, fc, fd)
+
+        work() if flag is None else pl.when(flag)(work)
+
     partner(1, inner)
-    block_behind(0, on_time)
+    block_behind(0, early)
     partner(0, inner)
-    block_behind(1, on_time)
-    partner(0, turned & late)
-    partner(1, turned & late)
-    from_sibling(swap)
-    add(lax.select(swap, 1, 0))
-    partner(0, swap)
-    partner(1, swap)
-    block_behind(0, late)
-    block_behind(1, late)
-    from_sibling(keep)
-    add(lax.select(swap, 0, 1))
+    block_behind(1, early)
+    add((0, 1), 2, inner)
+    block_behind(0, inner & late)
+    block_behind(1, inner & late)
+    when(core == 0, *both(odd_own, "wait_recv"))
+    when(core == 1, *both(even_own, "wait_recv"))
+    add((2, 3), 0)
+    partner(0, turned)
+    partner(1, turned)
     for i, arrived in enumerate((on_y, on_x)):
         arrived.wait_recv()
         when(core == 1, odd_partner[i].start)
     when(core == 0, *both(odd_partner, "wait_recv"))
     when(core == 1, *both(even_partner, "wait_recv"))
-    add(2, True)
+    add((4, 5), 1, inner, True)
+    add((1, 4, 5), 1, turned, True)
+    when(at_once, to_ahead[0].wait_send)
     to_ahead[1].wait_send()
     when(turns, round_y[1].wait_send)
     when(straight, to_next_k[0].wait_send, on_y.wait_send)
@@ -334,16 +343,16 @@
 
 
 def shards(orbitals, coulomb):
-    field = (TILES, 2 * NG, 128)
+    field, spare = (TILES, 2 * NG, 128), (TILES + 4, 2 * NG, 128)
     vmem = pltpu.VMEM
     total = pl.pallas_call(
         kernel,
-        out_shape=pltpu.VMEM(field, F32),
+        out_shape=pltpu.VMEM(spare, F32),
         in_specs=[pl.BlockSpec(memory_space=pl.ANY)] * 3,
         out_specs=pl.BlockSpec(memory_space=pltpu.VMEM),
         scratch_shapes=[
-            vmem((2, 64000), BF16), vmem((2, 64000), F32), vmem((960, 256), BF16), vmem(field, F32), vmem(field, F32),
-            vmem((14, 48, 128), F32), vmem((6, *field), BF16), vmem(field, BF16), vmem((3, ROWS, 128), F32),
+            vmem((2, 64000), BF16), vmem((2, 64000), F32), vmem((1120, 256), BF16), vmem(spare, F32), vmem(spare, F32),
+            vmem((TILES + 4, 48, 128), F32), vmem((6, *field), BF16), vmem(field, BF16), vmem((3, ROWS, 128), F32),
             vmem((ROWS, 256), BF16), vmem((2, 1600, 128), F32), vmem((2, 1600, 128), F32), vmem((ROWS, 256), BF16),
             pltpu.SemaphoreType.DMA((3,)), pltpu.SemaphoreType.DMA((24,)), pltpu.SemaphoreType.DMA((28,)),
         ],
@@ -354,7 +363,7 @@
         out_shape=jax.ShapeDtypeStruct(orbitals.shape, F32),
         in_specs=[pl.BlockSpec(memory_space=pltpu.VMEM)],
         out_specs=pl.BlockSpec(memory_space=pl.ANY),
-        scratch_shapes=[vmem((14, 48, 128), F32), vmem((2, 64000), F32), pltpu.SemaphoreType.DMA((4,))],
+        scratch_shapes=[vmem((TILES + 4, 48, 128), F32), vmem((2, 64000), F32), pltpu.SemaphoreType.DMA((4,))],
         compiler_params=pltpu.CompilerParams(vmem_limit_bytes=16 << 20),
     )(total)
 

time: 27 us -> 26 us (0.963)
  the two profiles are of different devices: /device:TPU:4 before, /device:TPU:1 now
where the time goes in v4:
time: 26 us; the launch traced here: 25.9 us
  Pallas kernels  25.9 us (100%)
    pallas_call x1, Pallas kernels, shards(): pl.pallas_call(kernel, out_shape=pltpu.VMEM(spare, F32), in_specs=[pl.Blo...  24.8 us
    pallas_call x1, Pallas kernels, shards(): pl.pallas_call(write, out_shape=jax.ShapeDtypeStruct(orbitals.shape, F32)...  1.04 us

profile of v4, /device:TPU:1, one launch (start us, length us, event | category | flops | bytes accessed | tf_op | source)
XLA Modules:
  0.0 25.9 jit_solution(1178174775056099228)
XLA Ops:
  0.0 24.8 %shard_map.37.total = f32[17,80,128]{2,1,0:T(8,128)S(1)} custom-call(bf16[1,1,2,64000]{3,2,1,0:T(2,128)(2,1)} %orbitals.1, f32[1,2,64000]{2,1,0:T(2,128)} %coulomb.1, bf16[1120,256]{1,0:T(8,128)(2,1)} %constant.2.clone.tables_ref), custom_call_target="tpu_custom_call" | custom-call | tf_op jit(solution)/shard_map/pallas_call | solution.py:348
  24.8 1.0 %shard_map.38 = f32[1,1,2,64000]{3,2,1,0:T(2,128)} custom-call(f32[17,80,128]{2,1,0:T(8,128)S(1)} %shard_map.37.total), custom_call_target="tpu_custom_call" | custom-call | tf_op jit(solution)/shard_map/pallas_call | solution.py:361

commit v5 on v4

--- a/solution.py
+++ b/solution.py
@@ -22,7 +22,7 @@
 MESH = pl.DeviceIdType.MESH
 TILES = 13
 ROWS = TILES * 128
-CHUNKS = ((0, 7), (7, 6))
+CHUNKS = ((0, 5), (5, 8))
 
 
 def tables():

time: 26 us -> 25.3 us (0.973)
  Pallas kernels: 25.9 us -> 25.1 us
    pallas_call x1, Pallas kernels: 24.8 us -> 24.1 us  [shards(): pl.pallas_call(kernel, out_shape=pltpu.VMEM(spare, F32), in_specs=[pl.Blo...]
where the time goes in v5:
time: 25.3 us; the launch traced here: 25.2 us
  Pallas kernels  25.1 us (99%)
    pallas_call x1, Pallas kernels, shards(): pl.pallas_call(kernel, out_shape=pltpu.VMEM(spare, F32), in_specs=[pl.Blo...  24.1 us
    pallas_call x1, Pallas kernels, shards(): pl.pallas_call(write, out_shape=jax.ShapeDtypeStruct(orbitals.shape, F32)...  1.04 us

profile of v5, /device:TPU:1, one launch (start us, length us, event | category | flops | bytes accessed | tf_op | source)
XLA Modules:
  0.0 25.2 jit_solution(7662116525662322384)
XLA Ops:
  0.0 24.1 %shard_map.37.total = f32[17,80,128]{2,1,0:T(8,128)S(1)} custom-call(bf16[1,1,2,64000]{3,2,1,0:T(2,128)(2,1)} %orbitals.1, f32[1,2,64000]{2,1,0:T(2,128)} %coulomb.1, bf16[1120,256]{1,0:T(8,128)(2,1)} %constant.2.clone.tables_ref), custom_call_target="tpu_custom_call" | custom-call | tf_op jit(solution)/shard_map/pallas_call | solution.py:348
  24.1 1.0 %shard_map.38 = f32[1,1,2,64000]{3,2,1,0:T(2,128)} custom-call(f32[17,80,128]{2,1,0:T(8,128)S(1)} %shard_map.37.total), custom_call_target="tpu_custom_call" | custom-call | tf_op jit(solution)/shard_map/pallas_call | solution.py:361

commit v6 on v5

--- a/solution.py
+++ b/solution.py
@@ -262,11 +262,11 @@
     total[:TILES] = jnp.zeros((TILES, 2 * NG, 128), F32)
     loads[1].wait()
     matrix_from_flat(kernel_flat, kernel_matrix, odd)
-    loads[2].wait()
-    spread_coulomb(kernel_matrix, tab, scale)
     when(turns, round_y[0].wait_send, round_y[1].start)
     when(straight, to_next_k[1].wait_send, to_next_k[0].start)
     when(jnp.logical_not(at_once), to_ahead[0].wait_send, to_ahead[1].start)
+    loads[2].wait()
+    spread_coulomb(kernel_matrix, tab, scale)
     @pl.when(turned)
     def _():
         terms(vis.at[0], [vis.at[0]], scale.at[0], tab, total, False, fa, fb, fc, fd)

time: 25.3 us -> 26.3 us (1.040)
  Pallas kernels: 25.1 us -> 26.2 us
    pallas_call x1, Pallas kernels: 24.1 us -> 25.1 us  [shards(): pl.pallas_call(kernel, out_shape=pltpu.VMEM(spare, F32), in_specs=[pl.Blo...]
where the time goes in v6:
time: 26.3 us; the launch traced here: 26.2 us
  Pallas kernels  26.2 us (100%)
    pallas_call x1, Pallas kernels, shards(): pl.pallas_call(kernel, out_shape=pltpu.VMEM(spare, F32), in_specs=[pl.Blo...  25.1 us
    pallas_call x1, Pallas kernels, shards(): pl.pallas_call(write, out_shape=jax.ShapeDtypeStruct(orbitals.shape, F32)...  1.04 us

profile of v6, /device:TPU:1, one launch (start us, length us, event | category | flops | bytes accessed | tf_op | source)
XLA Modules:
  0.0 26.2 jit_solution(3657552417786113746)
XLA Ops:
  0.0 25.1 %shard_map.37.total = f32[17,80,128]{2,1,0:T(8,128)S(1)} custom-call(bf16[1,1,2,64000]{3,2,1,0:T(2,128)(2,1)} %orbitals.1, f32[1,2,64000]{2,1,0:T(2,128)} %coulomb.1, bf16[1120,256]{1,0:T(8,128)(2,1)} %constant.2.clone.tables_ref), custom_call_target="tpu_custom_call" | custom-call | tf_op jit(solution)/shard_map/pallas_call | solution.py:348
  25.1 1.0 %shard_map.38 = f32[1,1,2,64000]{3,2,1,0:T(2,128)} custom-call(f32[17,80,128]{2,1,0:T(8,128)S(1)} %shard_map.37.total), custom_call_target="tpu_custom_call" | custom-call | tf_op jit(solution)/shard_map/pallas_call | solution.py:361
